TPU v7x, 32 devices: a whole 2x2x4 slice. The times are simulated.
32 devices in a mesh: gx: 4 (over y, core), gy: 8 (over z, x).
Axes of the slice: x: 2, y: 2, z: 4, core: 2. Of those that a mesh axis runs over, the one named last changes fastest.
Arguments:
- tiles: float32 [2, 3, 16384, 128], P(None, None, ('gx', 'gy')), may hold values from -6 to 6
- tile_owner: int32 [16384, 1], P(('gx', 'gy')), may hold values from 0 to 31; in each aligned block of 512 rows (0 to 511, 512 to 1023, ...) at most 32 rows name the same one
- tile_slot: int32 [16384], P(('gx', 'gy')), may hold values from 0 to 1023
- tile_count: int32 [32], P(('gx', 'gy')), may hold values from 384 to 512, as said below
- green: float32 [2, 6, 1, 2048, 2048], P(None, None, None, ('gx', 'gy')), may hold values from -6 to 6
Outputs:
- field_hat: float32 [2, 3, 1, 2048, 2048], P(None, None, None, ('gx', 'gy'))
Inputs may be any that keep to these rules, and one draw needn't show every extreme that they name: `tile_owner`: within the 512 entries of one device, live or not, no owner is named by more than 32; that many is reached. `tile_count`: some device has all 512 entries live.
All inputs are finite; a program needn't handle non-finite values.
Results may differ from a plain program's by a relative error of at most 0.00007.
Values sent between devices are 32-bit elements; how exact they have to be, the bound alone decides.
No kernel may reach another device: no remote copies, remote signals or barrier semaphores. Data moves between devices by JAX's collectives and lax.ppermute only.
A program may use at most 128 MiB of HBM per device.

v0:
```python
import functools
import math

import jax
import jax.numpy as jnp
import ml_dtypes
import numpy as np
from jax import lax
from jax.experimental import pallas as pl
from jax.experimental.pallas import tpu as pltpu
from jax.sharding import PartitionSpec as P

pair_index = ((0, 3, 4), (3, 1, 5), (4, 5, 2))
by_rows = (((1,), (1,)), ((), ()))


def params(mebibytes):
    return pltpu.CompilerParams(vmem_limit_bytes=mebibytes * 1024 * 1024)


def in_hbm(array):
    return pltpu.with_memory_space_constraint(array, pltpu.HBM)


def in_vmem(array):
    return pltpu.with_memory_space_constraint(array, pltpu.VMEM)


def cost(flops, moved):
    return pl.CostEstimate(flops=flops, bytes_accessed=moved, transcendentals=0)


def angles(rows, columns, length):
    products = np.outer(np.arange(rows), np.arange(columns)) % length
    return 2.0 * math.pi / length * products


def halves(table):
    wide = np.asarray(table, np.float32)
    high = wide.astype(ml_dtypes.bfloat16)
    low = (wide - high.astype(np.float32)).astype(ml_dtypes.bfloat16)
    return jnp.asarray(high), jnp.asarray(low)


def split_two(data):
    high = data.astype(jnp.bfloat16)
    return high, (data - high.astype(jnp.float32)).astype(jnp.bfloat16)


def split_three(data):
    high = data.astype(jnp.bfloat16)
    rest = data - high.astype(jnp.float32)
    middle = rest.astype(jnp.bfloat16)
    return high, middle, (rest - middle.astype(jnp.float32)).astype(jnp.bfloat16)


def dot_rows(left, right):
    return lax.dot_general(left, right, by_rows, preferred_element_type=jnp.float32)


def dot_rows_split(table, data):
    rows, depth = table.shape
    table_high, table_low = split_two(table)
    high, low = split_two(data)
    if depth > 128:
        both = dot_rows(jnp.concatenate([table_high, table_low]), high)
        return both[:rows] + both[rows:] + dot_rows(table_high, low)
    left = jnp.concatenate(
        [
            jnp.concatenate([table_high, table_high], axis=1),
            jnp.concatenate([table_low, jnp.zeros_like(table_low)], axis=1),
        ]
    )
    both = dot_rows(left, jnp.concatenate([high, low], axis=1))
    return both[:rows] + both[rows:]


def flat_fft(values, times):
    length = len(values)
    if length == 1:
        return values
    even = flat_fft(values[0::2], times)
    odd = flat_fft(values[1::2], times)
    lower, upper = [], []
    for k in range(length // 2):
        turned = times(odd[k], k, length)
        lower.append(jax.tree.map(lambda a, b: a + b, even[k], turned))
        upper.append(jax.tree.map(lambda a, b: a - b, even[k], turned))
    return lower + upper


def times_pair(value, k, length):
    real, imag = value
    if k == 0:
        return value
    if 4 * k == length:
        return (imag, -real)
    cos_k = math.cos(2.0 * math.pi * k / length)
    sin_k = math.sin(2.0 * math.pi * k / length)
    return (real * cos_k + imag * sin_k, imag * cos_k - real * sin_k)


def place_of(owner, count_gl):
    shift = count_gl.bit_length() - 1
    z = (owner >> shift) & 3
    return (((owner >> (shift + 2)) << shift) + (owner & (count_gl - 1))) * 4 + z


def owner_order(devices, count_gl):
    order = [0] * devices
    for owner in range(devices):
        order[place_of(owner, count_gl)] = owner
    return order


def pack_kernel(
    devices, count_gl, per_owner, count, me, owner_row, slot_row, tiles, out, *scratch
):
    held, made, lists, sems, out_sems = scratch
    comps = tiles.shape[1]
    listed = owner_row.shape[1]
    fetches = [
        pltpu.make_async_copy(owner_row, lists.at[0], sems.at[0]),
        pltpu.make_async_copy(slot_row, lists.at[1], sems.at[1]),
    ]
    fetches += [
        pltpu.make_async_copy(tiles.at[:, comp], held.at[i], sems.at[2 + i])
        for i, comp in enumerate(range(comps))
    ]
    for fetch in fetches:
        fetch.start()
    fetches[0].wait()
    live_count = count[0]
    live = lax.broadcasted_iota(jnp.int32, (1, listed), 1) < live_count
    place = jnp.where(live, place_of(lists[0], count_gl), -1)
    place_at = lax.broadcasted_iota(jnp.int32, (devices, listed), 0)
    named = jnp.where(place_at == place, 1.0, 0.0)
    sender = lax.broadcasted_iota(jnp.int32, (listed, listed), 0)
    reader = lax.broadcasted_iota(jnp.int32, (listed, listed), 1)
    before = jnp.where(sender < reader, 1.0, 0.0).astype(jnp.bfloat16)
    counted = jnp.dot(named.astype(jnp.bfloat16), before, preferred_element_type=jnp.float32)
    rank = jnp.sum(counted * named, axis=0, keepdims=True).astype(jnp.int32)
    target = jnp.where(live, place * per_owner + rank, -1)
    target_at = lax.broadcasted_iota(jnp.int32, (devices * per_owner, listed), 0)
    chosen = jnp.where(target_at == target, 1.0, 0.0).astype(jnp.bfloat16)
    fetches[1].wait()
    sends = []

    def send(start, rows):
        part = pl.ds(start, rows)
        copy = pltpu.make_async_copy(
            made.at[:, part], out.at[:, part], out_sems.at[len(sends)]
        )
        copy.start()
        sends.append(copy)

    stated = lists[1] + 1
    lane = rank + (place_of(me[0], count_gl) & (128 // per_owner - 1)) * per_owner
    lane_at = lax.broadcasted_iota(jnp.int32, (128, listed), 0)
    ranked = jnp.where(lane_at == lane, 1.0, 0.0).astype(jnp.bfloat16)
    coarse = (named * (stated >> 5).astype(jnp.float32)).astype(jnp.bfloat16)
    fine = (named * (stated & 31).astype(jnp.float32)).astype(jnp.bfloat16)
    slots = 32.0 * dot_rows(coarse, ranked) + dot_rows(fine, ranked)
    start = 2 * comps * per_owner
    made[:, start:, :] = jnp.broadcast_to(slots[:, None, :], (devices, 8, 128))
    send(start, 8)
    for comp in range(comps):
        fetches[2 + comp].wait()
        for r in range(2):
            parts = jnp.concatenate(split_three(held[comp, r]), axis=1)
            got = jnp.dot(chosen, parts, preferred_element_type=jnp.float32)
            whole = (got[:, :128] + got[:, 128:256]) + got[:, 256:]
            start = (2 * comp + r) * per_owner
            made[:, start : start + per_owner, :] = whole.reshape(devices, per_owner, 128)
            send(start, per_owner)
    for copy in sends:
        copy.wait()


def pack(tiles, owner_row, slot_row, count, me, devices, count_gl, per_owner):
    comps, listed = tiles.shape[1:3]
    rows = 2 * comps * per_owner + 8
    return pl.pallas_call(
        functools.partial(pack_kernel, devices, count_gl, per_owner),
        out_shape=pltpu.HBM((devices, rows, 128), jnp.float32),
        in_specs=[pl.BlockSpec(memory_space=pltpu.SMEM)] * 2
        + [pl.BlockSpec(memory_space=pltpu.HBM)] * 3,
        out_specs=pl.BlockSpec(memory_space=pltpu.HBM),
        scratch_shapes=[
            pltpu.VMEM((comps, 2, listed, 128), jnp.float32),
            pltpu.VMEM((devices, rows, 128), jnp.float32),
            pltpu.VMEM((2, 1, listed), jnp.int32),
            pltpu.SemaphoreType.DMA((2 + comps,)),
            pltpu.SemaphoreType.DMA((1 + 2 * comps,)),
        ],
        compiler_params=params(24),
        cost_estimate=cost(
            devices * per_owner * listed * 768 * 2 * comps, devices * rows * 1024
        ),
    )(count, me, *[in_hbm(a) for a in (owner_row, slot_row, tiles)])


def slab_kernel(comps, x_local, blocks, per_owner, table, twist, data, out, *scratch):
    made, slab, turned, out_sems = scratch
    devices = data.shape[0]
    entries = devices * per_owner
    y_local = blocks * 128 // devices
    wide = 2 * x_local
    shift = blocks.bit_length() - 1
    every = 128 // per_owner
    stated = [
        sum([data[o, data.shape[1] - 8 :][:1] for o in range(start, start + every)])
        for start in range(0, devices, every)
    ]
    slot = jnp.concatenate(stated, axis=1).astype(jnp.int32) - 1
    landing = jnp.where(slot >= 0, (slot & (blocks - 1)) * x_local + (slot >> shift), -1)
    parts = []
    for comp in comps:
        for r in range(2):
            start = (2 * comp + r) * per_owner
            one = data[:, start : start + per_owner, :]
            parts.extend(split_two(one.reshape(entries, 128)))
    parts = jnp.concatenate(parts, axis=1)
    for start in range(0, blocks * x_local, 256):
        place = start + lax.broadcasted_iota(jnp.int32, (256, entries), 0)
        chosen = jnp.where(place == landing, 1.0, 0.0).astype(jnp.bfloat16)
        got = jnp.dot(chosen, parts, preferred_element_type=jnp.float32)
        for i in range(2 * len(comps)):
            slab[i // 2, i % 2, start : start + 256, :] = (
                got[:, 256 * i : 256 * i + 128] + got[:, 256 * i + 128 : 256 * i + 256]
            )
    sends = []
    for index in range(len(comps)):

        @pl.loop(0, x_local // 8)
        def _(step):
            at = pl.multiple_of(step * 8, 8)
            values = [
                tuple(slab[index, r, pl.ds(t * x_local + at, 8), :] for r in range(2))
                for t in range(blocks)
            ]
            waves = flat_fft(values, times_pair)
            for k in range(blocks):
                real, imag = waves[k]
                cos_k, sin_k = twist[0, k : k + 1, :], twist[1, k : k + 1, :]
                new_real = real * cos_k + imag * sin_k
                new_imag = imag * cos_k - real * sin_k
                first = pl.ds(k * wide + at, 8)
                second = pl.ds(k * wide + x_local + at, 8)
                turned[first, :128] = new_real
                turned[first, 128:] = new_imag
                turned[second, :128] = new_imag
                turned[second, 128:] = -new_real

        together = 4
        for start in range(0, blocks, together):
            moved = dot_rows_split(
                table[...], turned[start * wide : (start + together) * wide, :]
            )
            for k in range(start, start + together):
                one = moved[:, (k - start) * wide : (k - start + 1) * wide]
                made[index, pl.ds(k, 128, stride=blocks), :] = one
        send = pltpu.make_async_copy(
            made.at[index].reshape(devices, y_local, wide),
            out.at[:, pl.ds(index * y_local, y_local)],
            out_sems.at[index],
        )
        send.start()
        sends.append(send)
    for send in sends:
        send.wait()


def slab_waves(comps, data, x_local, blocks, count_gl, per_owner):
    devices = data.shape[0]
    y_cells = blocks * 128
    y_local = y_cells // devices
    fine = angles(128, 128, 128)
    table = np.concatenate([np.cos(fine), np.sin(fine)], axis=1).astype(np.float32)
    order = owner_order(devices, count_gl)
    table = table.reshape(devices, 128 // devices, 256)[order].reshape(128, 256)
    twist_angle = angles(blocks, 128, y_cells)
    twist = np.stack([np.cos(twist_angle), np.sin(twist_angle)]).astype(np.float32)
    entries = devices * per_owner
    count = len(comps)
    return pl.pallas_call(
        functools.partial(slab_kernel, comps, x_local, blocks, per_owner),
        out_shape=pltpu.HBM((devices, count * y_local, 2 * x_local), jnp.float32),
        in_specs=[pl.BlockSpec(memory_space=pltpu.VMEM)] * 3,
        out_specs=pl.BlockSpec(memory_space=pltpu.HBM),
        scratch_shapes=[
            pltpu.VMEM((count, y_cells, 2 * x_local), jnp.float32),
            pltpu.VMEM((count, 2, blocks * x_local, 128), jnp.float32),
            pltpu.VMEM((blocks * 2 * x_local, 256), jnp.float32),
            pltpu.SemaphoreType.DMA((count,)),
        ],
        compiler_params=params(24),
        cost_estimate=cost(
            count * (blocks * x_local * entries * 1024 + y_cells * x_local * 3072),
            count * (entries * 1024 + y_cells * x_local * 8),
        ),
    )(jnp.asarray(table), jnp.asarray(twist), in_vmem(data))


def swap_parts(value, x_local):
    if 2 * x_local == 128:
        return pltpu.roll(value, x_local, 1)
    return jnp.concatenate([value[:, x_local:], value[:, :x_local]], axis=1)


def x_steps(
    devices, x_local, y_local, order, index, twist, table, data, turned, columns, store
):
    wide = 2 * x_local
    lane = lax.broadcasted_iota(jnp.int32, (1, wide), 1)
    sign = jnp.where(lane < x_local, 1.0, -1.0)

    def times(value, k, length):
        if k == 0:
            return value
        swapped = swap_parts(value, x_local) * sign
        if 4 * k == length:
            return swapped
        cos_k = math.cos(2.0 * math.pi * k / length)
        sin_k = math.sin(2.0 * math.pi * k / length)
        return value * cos_k + swapped * sin_k

    @pl.loop(0, y_local // 8)
    def _(step):
        at = pl.multiple_of(step * 8, 8)
        rows = pl.ds(index * y_local + at, 8)
        values = [data[order.index(o), rows, :] for o in range(devices)]
        waves = flat_fft(values, times)
        for k in range(devices):
            swapped = swap_parts(waves[k], x_local)
            new = waves[k] * twist[0, k : k + 1, :] + swapped * twist[1, k : k + 1, :]
            turned[k, pl.ds(at, 8), :] = new
            turned[k, pl.ds(y_local + at, 8), :] = swap_parts(new, x_local) * sign

    together = 4
    for start in range(0, devices, together):
        stacked = turned[start : start + together].reshape(together * 2 * y_local, wide)
        moved = dot_rows_split(table[...], stacked)
        for k in range(start, start + together):
            columns[pl.ds(k, x_local, stride=devices), :] = moved[
                :, (k - start) * 2 * y_local : (k - start + 1) * 2 * y_local
            ]
    for start in range(0, devices * x_local, 128):
        store(start, columns[start : start + 128, :].T)


def x_kernel(devices, x_local, y_local, order, index, twist, table, data, out, *scratch):
    made, out_sem = scratch[:2]

    def store(start, block):
        made[0, :, start : start + 128] = block[:y_local]
        made[1, :, start : start + 128] = block[y_local:]

    x_steps(
        devices, x_local, y_local, order, index, twist, table, data, *scratch[2:], store
    )
    send = pltpu.make_async_copy(made, out, out_sem)
    send.start()
    send.wait()


def last_kernel(devices, x_local, y_local, order, index, twist, table, data, *refs):
    green, first, second, out = refs[:4]
    scratch, (tensor, kept, made, in_sems, out_sems) = refs[4:6], refs[6:]
    x_cells = devices * x_local
    pieces = made.shape[0]
    width = x_cells // pieces
    fetches = [
        pltpu.make_async_copy(first, kept.at[0], in_sems.at[0]),
        pltpu.make_async_copy(second, kept.at[1], in_sems.at[1]),
        pltpu.make_async_copy(green, tensor, in_sems.at[2]),
    ]
    for fetch in fetches:
        fetch.start()

    def store(start, block):
        kept[2, 0, :, start : start + 128] = block[:y_local]
        kept[2, 1, :, start : start + 128] = block[y_local:]

    x_steps(devices, x_local, y_local, order, index, twist, table, data, *scratch, store)
    for fetch in fetches:
        fetch.wait()
    sends = []
    for piece in range(pieces):

        @pl.loop(0, y_local // 8)
        def _(step):
            rows = pl.ds(pl.multiple_of(step * 8, 8), 8)
            columns = pl.ds(piece * width, width)
            waves = [(kept[c, 0, rows, columns], kept[c, 1, rows, columns]) for c in range(3)]
            sums = [[None, None] for _ in range(3)]
            for entry in range(6):
                green_real = tensor[0, entry, rows, columns]
                green_imag = tensor[1, entry, rows, columns]
                for row in range(3):
                    for col in range(3):
                        if pair_index[row][col] != entry:
                            continue
                        real, imag = waves[col]
                        real_term = green_real * real - green_imag * imag
                        imag_term = green_real * imag + green_imag * real
                        old = sums[row]
                        sums[row] = [
                            real_term if old[0] is None else old[0] + real_term,
                            imag_term if old[1] is None else old[1] + imag_term,
                        ]
            for row in range(3):
                made[piece, 0, row, rows, :] = sums[row][0]
                made[piece, 1, row, rows, :] = sums[row][1]

        send = pltpu.make_async_copy(
            made.at[piece],
            out.at[:, :, :, pl.ds(piece * width, width)],
            out_sems.at[piece],
        )
        send.start()
        sends.append(send)
    for send in sends:
        send.wait()


def x_tables(devices, x_local, y_cells):
    x_cells = devices * x_local
    fine = angles(x_local, x_local, x_local)
    scale = 1.0 / math.sqrt(x_cells * y_cells)
    table = np.concatenate([np.cos(fine), np.sin(fine)], axis=1) * scale
    angle = angles(devices, x_local, x_cells)
    cos_a, sin_a = np.cos(angle), np.sin(angle)
    twist = np.stack(
        [np.concatenate([cos_a, cos_a], axis=1), np.concatenate([sin_a, -sin_a], axis=1)]
    )
    return jnp.asarray(twist.astype(np.float32)), jnp.asarray(table.astype(np.float32))


def x_scratch(devices, x_local, y_local):
    return [
        pltpu.VMEM((devices, 2 * y_local, 2 * x_local), jnp.float32),
        pltpu.VMEM((devices * x_local, 2 * y_local), jnp.float32),
    ]


def x_waves(index, data, devices, x_local, y_local, y_cells, count_gl):
    x_cells = devices * x_local
    order = owner_order(devices, count_gl)
    return pl.pallas_call(
        functools.partial(x_kernel, devices, x_local, y_local, order, index),
        out_shape=pltpu.HBM((2, y_local, x_cells), jnp.float32),
        in_specs=[pl.BlockSpec(memory_space=pltpu.VMEM)] * 3,
        out_specs=pl.BlockSpec(memory_space=pltpu.HBM),
        scratch_shapes=[
            pltpu.VMEM((2, y_local, x_cells), jnp.float32),
            pltpu.SemaphoreType.DMA(()),
        ]
        + x_scratch(devices, x_local, y_local),
        compiler_params=params(24),
        cost_estimate=cost(x_cells * y_local * x_local * 24, x_cells * y_local * 16),
    )(*x_tables(devices, x_local, y_cells), in_vmem(data))


def last_waves(index, data, green, first, second, devices, x_local, y_local, y_cells, count_gl):
    x_cells = devices * x_local
    order = owner_order(devices, count_gl)
    pieces = 8
    return pl.pallas_call(
        functools.partial(last_kernel, devices, x_local, y_local, order, index),
        out_shape=pltpu.HBM((2, 3, y_local, x_cells), jnp.float32),
        in_specs=[pl.BlockSpec(memory_space=pltpu.VMEM)] * 3
        + [pl.BlockSpec(memory_space=pltpu.HBM)] * 3,
        out_specs=pl.BlockSpec(memory_space=pltpu.HBM),
        scratch_shapes=x_scratch(devices, x_local, y_local)
        + [
            pltpu.VMEM((2, 6, y_local, x_cells), jnp.float32),
            pltpu.VMEM((3, 2, y_local, x_cells), jnp.float32),
            pltpu.VMEM((pieces, 2, 3, y_local, x_cells // pieces), jnp.float32),
            pltpu.SemaphoreType.DMA((3,)),
            pltpu.SemaphoreType.DMA((pieces,)),
        ],
        compiler_params=params(40),
        cost_estimate=cost(x_cells * y_local * (x_local * 24 + 72), x_cells * y_local * 96),
    )(
        *x_tables(devices, x_local, y_cells),
        in_vmem(data),
        *[in_hbm(a) for a in (green, first, second)],
    )


def gate_kernel(data, after, out):
    del data, after, out


def once_after(data, after):
    return pl.pallas_call(
        gate_kernel,
        out_shape=pltpu.HBM(data.shape, data.dtype),
        in_specs=[pl.BlockSpec(memory_space=pltpu.HBM), pl.BlockSpec(memory_space=pl.ANY)],
        out_specs=pl.BlockSpec(memory_space=pltpu.HBM),
        input_output_aliases={0: 0},
        compiler_params=params(1),
        cost_estimate=cost(0, 0),
    )(in_hbm(data), after)


def exchange(data):
    return lax.all_to_all(data, ("gx", "gl", "gz"), split_axis=0, concat_axis=0, tiled=True)


def per_device(tiles, tile_owner, tile_slot, tile_count, green):
    count_gl = lax.axis_size("gl")
    devices = lax.axis_size("gx") * 4 * count_gl
    tile_total, tile_len = tiles.shape[2], tiles.shape[3]
    planes, y_local, x_cells = green.shape[2:]
    y_cells = y_local * devices
    x_local = x_cells // devices
    blocks = y_cells // tile_len
    per_owner = max(2, 2 * tile_total // devices)
    assert planes == 1 and tile_len == 128
    owner_row, slot_row = tile_owner.reshape(1, tile_total), tile_slot.reshape(1, tile_total)
    green = green.reshape(2, 6, y_local, x_cells)
    me = (lax.axis_index("gx") * 4 + lax.axis_index("gz")) * count_gl + lax.axis_index("gl")
    lists = (owner_row, slot_row, tile_count, me.reshape(1).astype(jnp.int32))
    arrived = exchange(pack(tiles, *lists, devices, count_gl, per_owner))
    grid = (x_local, blocks, count_gl, per_owner)
    early = exchange(slab_waves((0, 1), arrived, *grid))
    late = slab_waves((2,), arrived, *grid)
    late = exchange(once_after(late, early))
    sizes = (devices, x_local, y_local, y_cells, count_gl)
    waves = [x_waves(comp, early, *sizes) for comp in range(2)]
    mixed = last_waves(0, late, green, *waves, *sizes)
    return mixed.reshape(2, 3, planes, y_local, x_cells)


def solution(mesh):
    count_gx, count_gy = mesh.devices.shape
    fine_mesh = jax.sharding.Mesh(
        mesh.devices.reshape(count_gx, 4, count_gy // 4), ("gx", "gz", "gl")
    )
    every = ("gx", "gz", "gl")
    in_specs = (
        P(None, None, every, None),
        P(every, None),
        P(every),
        P(every),
        P(None, None, None, every, None),
    )
    out_specs = P(None, None, None, every, None)
    return jax.shard_map(
        per_device, mesh=fine_mesh, in_specs=in_specs, out_specs=out_specs, check_vma=False
    )
```

profile of v0, /device:TPU:0, one launch (start us, length us, event | category | flops | bytes accessed | tf_op | source)
XLA Modules:
  0.0 186.6 jit_solution(13109680271933691099)
XLA Ops:
  0.7 6.1 %shard_map.145 = f32[32,200,128]{2,1,0:T(8,128)} custom-call(s32[1]{0:T(128)S(6)} %copy.19.count, s32[1]{0:T(128)} %bitcast.me, s32[1,512]{1,0:T(1,128)} %bitcast.8, s32[1,512]{1,0:T(1,128)} %bitcast.9, f32[2,3,512,128]{3,2,1,0:T(8,128)} %tiles.1), custom_call_target="tpu_custom_call" | custom-call | flops 2415919104 | bytes 6553600 | tf_op jit(solution)/shard_map/pallas_call | solution.py:183
  6.8 0.0 copy-start.4
  6.8 0.0 copy-start.5
  6.8 82.9 %all_to_all.15.data = f32[32,200,128]{2,1,0:T(8,128)S(1)} all-to-all(f32[32,200,128]{2,1,0:T(8,128)} %shard_map.145), channel_id=1, replica_groups=mesh['gx'=4,'gz'=4,'gl'=2] {'gx','gl','gz'}, dimensions={0} | all-to-all | bytes 6553600 | tf_op jit(solution)/shard_map/all_to_all | solution.py:509
  89.7 0.0 copy-done.4
  89.7 0.0 copy-done.5
  89.7 6.2 %shard_map.147 = f32[32,128,128]{2,1,0:T(8,128)} custom-call(f32[128,256]{1,0:T(8,128)S(1)} %copy-done.4, f32[2,16,128]{2,1,0:T(8,128)S(1)} %copy-done.5, f32[32,200,128]{2,1,0:T(8,128)S(1)} %all_to_all.15.data), custom_call_target="tpu_custom_call" | custom-call | flops 2952790016 | bytes 4194304 | tf_op jit(solution)/shard_map/pallas_call | solution.py:286
  96.0 0.0 copy-start
  96.0 1.7 copy-done
  97.6 2.7 %all-to-all-start.1 = ((f32[32,128,128]{2,1,0:T(8,128)}), f32[32,128,128]{2,1,0:T(8,128)S(1)}, u32[]{:S(2)}, u32[]{:S(2)}) async-start(f32[32,128,128]{2,1,0:T(8,128)} %shard_map.147), calls=%async_computation.1 | async-start | bytes 4194304 | tf_op jit(solution)/shard_map/all_to_all | solution.py:509
  100.4 0.0 copy-start.1
  100.4 1.9 %copy-done.1 = f32[32,200,128]{2,1,0:T(8,128)S(1)} copy-done((f32[32,200,128]{2,1,0:T(8,128)S(1)}, f32[32,200,128]{2,1,0:T(8,128)}, u32[]{:S(2)}) %copy-start.1) | copy-done | bytes 3276824
  102.3 3.7 %shard_map.146.data = f32[32,64,128]{2,1,0:T(8,128)} custom-call(f32[128,256]{1,0:T(8,128)S(1)} %copy-done.4, f32[2,16,128]{2,1,0:T(8,128)S(1)} %copy-done.5, f32[32,200,128]{2,1,0:T(8,128)S(1)} %copy-done.1), custom_call_target="tpu_custom_call" | custom-call | flops 1476395008 | bytes 2097152 | tf_op jit(solution)/shard_map/pallas_call | solution.py:286
  106.0 0.0 copy-start.2
  106.0 0.0 copy-start.3
  106.1 43.0 %all-to-all-done.1.after.data = f32[32,128,128]{2,1,0:T(8,128)S(1)} async-done(((f32[32,128,128]{2,1,0:T(8,128)}), f32[32,128,128]{2,1,0:T(8,128)S(1)}, u32[]{:S(2)}, u32[]{:S(2)}) %all-to-all-start.1) | async-done | bytes 2097184 | tf_op jit(solution)/shard_map/all_to_all | solution.py:509
  149.1 3.0 %all-to-all-start.2 = ((f32[32,64,128]{2,1,0:T(8,128)}), f32[32,64,128]{2,1,0:T(8,128)S(1)}, u32[]{:S(2)}, u32[]{:S(2)}) async-start(f32[32,64,128]{2,1,0:T(8,128)} %shard_map.148), calls=%async_computation.2 | async-start | bytes 2097152 | tf_op jit(solution)/shard_map/all_to_all | solution.py:509
  152.0 0.0 copy-done.2
  152.0 0.0 copy-done.3
  152.0 6.4 %shard_map.150.refs_2_ = f32[2,64,2048]{2,1,0:T(8,128)} custom-call(f32[2,32,128]{2,1,0:T(8,128)S(1)} %copy-done.3, f32[64,128]{1,0:T(8,128)S(1)} %copy-done.2, f32[32,128,128]{2,1,0:T(8,128)S(1)} %all-to-all-done.1.after.data), custom_call_target="tpu_custom_call" | custom-call | flops 201326592 | bytes 2097152 | tf_op jit(solution)/shard_map/pallas_call | solution.py:450
  158.4 6.3 %shard_map.149.refs_1_ = f32[2,64,2048]{2,1,0:T(8,128)} custom-call(f32[2,32,128]{2,1,0:T(8,128)S(1)} %copy-done.3, f32[64,128]{1,0:T(8,128)S(1)} %copy-done.2, f32[32,128,128]{2,1,0:T(8,128)S(1)} %all-to-all-done.1.after.data), custom_call_target="tpu_custom_call" | custom-call | flops 201326592 | bytes 2097152 | tf_op jit(solution)/shard_map/pallas_call | solution.py:450
  164.7 13.9 %all-to-all-done.2.data = f32[32,64,128]{2,1,0:T(8,128)S(1)} async-done(((f32[32,64,128]{2,1,0:T(8,128)}), f32[32,64,128]{2,1,0:T(8,128)S(1)}, u32[]{:S(2)}, u32[]{:S(2)}) %all-to-all-start.2) | async-done | bytes 1048608 | tf_op jit(solution)/shard_map/all_to_all | solution.py:509
  178.6 7.9 %shard_map.151 = f32[2,3,64,2048]{3,2,1,0:T(8,128)} custom-call(f32[2,32,128]{2,1,0:T(8,128)S(1)} %copy-done.3, f32[64,128]{1,0:T(8,128)S(1)} %copy-done.2, f32[32,64,128]{2,1,0:T(8,128)S(1)} %all-to-all-done.2.data, f32[2,6,64,2048]{3,2,1,0:T(8,128)} %bitcast.7, f32[2,64,2048]{2,1,0:T(8,128)} %shard_map.149.refs_1_, f32[2,64,2048]{2,1,0:T(8,128)} %shard_map.150.refs_2_), custom_call_target="tpu_custom_call" | custom-call | flops 210763776 | bytes 12582912 | tf_op jit(solution)/shard_map/pallas_call | solution.py:469
  (1 shorter events, 0.0 us)
Async XLA Ops:
  6.8 82.9 %copy-start.4 = (f32[128,256]{1,0:T(8,128)S(1)}, f32[128,256]{1,0:T(8,128)}, u32[]{:S(2)}) copy-start(f32[128,256]{1,0:T(8,128)} %constant.23.clone.table) | copy-start | bytes 393220
  6.8 82.9 %copy-start.5 = (f32[2,16,128]{2,1,0:T(8,128)S(1)}, f32[2,16,128]{2,1,0:T(8,128)}, u32[]{:S(2)}) copy-start(f32[2,16,128]{2,1,0:T(8,128)} %constant.24.clone.twist) | copy-start | bytes 49156
  96.0 1.7 copy-start
  97.6 51.4 %all-to-all-start.1 = ((f32[32,128,128]{2,1,0:T(8,128)}), f32[32,128,128]{2,1,0:T(8,128)S(1)}, u32[]{:S(2)}, u32[]{:S(2)}) async-start(f32[32,128,128]{2,1,0:T(8,128)} %shard_map.147), calls=%async_computation.1 | async-start | bytes 4194304 | tf_op jit(solution)/shard_map/all_to_all | solution.py:509
  100.4 1.9 %copy-start.1 = (f32[32,200,128]{2,1,0:T(8,128)S(1)}, f32[32,200,128]{2,1,0:T(8,128)}, u32[]{:S(2)}) copy-start(f32[32,200,128]{2,1,0:T(8,128)} %copy-done) | copy-start | bytes 9830404
  106.0 46.0 %copy-start.2 = (f32[64,128]{1,0:T(8,128)S(1)}, f32[64,128]{1,0:T(8,128)}, u32[]{:S(2)}) copy-start(f32[64,128]{1,0:T(8,128)} %constant.26.clone.table) | copy-start | bytes 98308
  106.0 46.0 %copy-start.3 = (f32[2,32,128]{2,1,0:T(8,128)S(1)}, f32[2,32,128]{2,1,0:T(8,128)}, u32[]{:S(2)}) copy-start(f32[2,32,128]{2,1,0:T(8,128)} %constant.25.clone.twist) | copy-start | bytes 98308
  149.1 29.6 %all-to-all-start.2 = ((f32[32,64,128]{2,1,0:T(8,128)}), f32[32,64,128]{2,1,0:T(8,128)S(1)}, u32[]{:S(2)}, u32[]{:S(2)}) async-start(f32[32,64,128]{2,1,0:T(8,128)} %shard_map.148), calls=%async_computation.2 | async-start | bytes 2097152 | tf_op jit(solution)/shard_map/all_to_all | solution.py:509
where the time goes:
time: 187 us
  blocking collectives  82.9 us (44%)
  waiting for transfers between devices  56.9 us (30%)
  Pallas kernels  36.6 us (20%)
  starting transfers between devices  5.69 us (3%)
  local copies, waits for them, and re-layouts  3.63 us (2%)
    all_to_all x1, blocking collectives, exchange(): lax.all_to_all(data, ('gx', 'gl', 'gz'), split_axis=0, concat_axis=0, til...  82.9 us
    all_to_all x2, waiting for transfers between devices, exchange(): lax.all_to_all(data, ('gx', 'gl', 'gz'), split_axis=0, concat_axis=0, til...  56.9 us
    pallas_call x2, Pallas kernels, x_waves(): pl.pallas_call(functools.partial(x_kernel, devices, x_local, y_local, ord...  12.7 us
    pallas_call x2, Pallas kernels, slab_waves(): pl.pallas_call(functools.partial(slab_kernel, comps, x_local, blocks, per...  9.96 us
    pallas_call x1, Pallas kernels, last_waves(): pl.pallas_call(functools.partial(last_kernel, devices, x_local, y_local,...  7.86 us
    pallas_call x1, Pallas kernels, pack(): pl.pallas_call(functools.partial(pack_kernel, devices, count_gl, per_owne...  6.1 us
    all_to_all x2, starting transfers between devices, exchange(): lax.all_to_all(data, ('gx', 'gl', 'gz'), split_axis=0, concat_axis=0, til...  5.69 us
  transfers between devices with their start and end apart: 2, of which 2 were waited for; matrix products, arithmetic and copies ran while one was open for 0% of the time, Pallas kernels for 9%

commit v1 on v0

--- a/solution.py
+++ b/solution.py
@@ -114,10 +114,9 @@
 
 
 def pack_kernel(
-    devices, count_gl, per_owner, count, me, owner_row, slot_row, tiles, out, *scratch
+    devices, count_gl, per_owner, comps, with_slots, count, me, owner_row, slot_row, tiles, *refs
 ):
-    held, made, lists, sems, out_sems = scratch
-    comps = tiles.shape[1]
+    out, held, made, lists, sems, out_sems = refs[-6:]
     listed = owner_row.shape[1]
     fetches = [
         pltpu.make_async_copy(owner_row, lists.at[0], sems.at[0]),
@@ -125,7 +124,7 @@
     ]
     fetches += [
         pltpu.make_async_copy(tiles.at[:, comp], held.at[i], sems.at[2 + i])
-        for i, comp in enumerate(range(comps))
+        for i, comp in enumerate(comps)
     ]
     for fetch in fetches:
         fetch.start()
@@ -154,83 +153,100 @@
         copy.start()
         sends.append(copy)
 
-    stated = lists[1] + 1
-    lane = rank + (place_of(me[0], count_gl) & (128 // per_owner - 1)) * per_owner
-    lane_at = lax.broadcasted_iota(jnp.int32, (128, listed), 0)
-    ranked = jnp.where(lane_at == lane, 1.0, 0.0).astype(jnp.bfloat16)
-    coarse = (named * (stated >> 5).astype(jnp.float32)).astype(jnp.bfloat16)
-    fine = (named * (stated & 31).astype(jnp.float32)).astype(jnp.bfloat16)
-    slots = 32.0 * dot_rows(coarse, ranked) + dot_rows(fine, ranked)
-    start = 2 * comps * per_owner
-    made[:, start:, :] = jnp.broadcast_to(slots[:, None, :], (devices, 8, 128))
-    send(start, 8)
-    for comp in range(comps):
-        fetches[2 + comp].wait()
+    if with_slots:
+        stated = lists[1] + 1
+        lane = rank + (place_of(me[0], count_gl) & (128 // per_owner - 1)) * per_owner
+        lane_at = lax.broadcasted_iota(jnp.int32, (128, listed), 0)
+        ranked = jnp.where(lane_at == lane, 1.0, 0.0).astype(jnp.bfloat16)
+        coarse = (named * (stated >> 5).astype(jnp.float32)).astype(jnp.bfloat16)
+        fine = (named * (stated & 31).astype(jnp.float32)).astype(jnp.bfloat16)
+        slots = 32.0 * dot_rows(coarse, ranked) + dot_rows(fine, ranked)
+        start = 2 * len(comps) * per_owner
+        made[:, start:, :] = jnp.broadcast_to(slots[:, None, :], (devices, 8, 128))
+        send(start, 8)
+    for i in range(len(comps)):
+        fetches[2 + i].wait()
         for r in range(2):
-            parts = jnp.concatenate(split_three(held[comp, r]), axis=1)
+            parts = jnp.concatenate(split_three(held[i, r]), axis=1)
             got = jnp.dot(chosen, parts, preferred_element_type=jnp.float32)
             whole = (got[:, :128] + got[:, 128:256]) + got[:, 256:]
-            start = (2 * comp + r) * per_owner
+            start = (2 * i + r) * per_owner
             made[:, start : start + per_owner, :] = whole.reshape(devices, per_owner, 128)
             send(start, per_owner)
     for copy in sends:
         copy.wait()
 
 
-def pack(tiles, owner_row, slot_row, count, me, devices, count_gl, per_owner):
-    comps, listed = tiles.shape[1:3]
-    rows = 2 * comps * per_owner + 8
+def pack(tiles, comps, owner_row, slot_row, count, me, after, devices, count_gl, per_owner):
+    listed = tiles.shape[2]
+    with_slots = after is None
+    rows = 2 * len(comps) * per_owner + (8 if with_slots else 0)
+    extra = () if with_slots else (after,)
     return pl.pallas_call(
-        functools.partial(pack_kernel, devices, count_gl, per_owner),
+        functools.partial(pack_kernel, devices, count_gl, per_owner, comps, with_slots),
         out_shape=pltpu.HBM((devices, rows, 128), jnp.float32),
         in_specs=[pl.BlockSpec(memory_space=pltpu.SMEM)] * 2
-        + [pl.BlockSpec(memory_space=pltpu.HBM)] * 3,
+        + [pl.BlockSpec(memory_space=pltpu.HBM)] * (3 + len(extra)),
         out_specs=pl.BlockSpec(memory_space=pltpu.HBM),
         scratch_shapes=[
-            pltpu.VMEM((comps, 2, listed, 128), jnp.float32),
+            pltpu.VMEM((len(comps), 2, listed, 128), jnp.float32),
             pltpu.VMEM((devices, rows, 128), jnp.float32),
             pltpu.VMEM((2, 1, listed), jnp.int32),
-            pltpu.SemaphoreType.DMA((2 + comps,)),
-            pltpu.SemaphoreType.DMA((1 + 2 * comps,)),
+            pltpu.SemaphoreType.DMA((2 + len(comps),)),
+            pltpu.SemaphoreType.DMA((1 + 2 * len(comps),)),
         ],
         compiler_params=params(24),
         cost_estimate=cost(
-            devices * per_owner * listed * 768 * 2 * comps, devices * rows * 1024
+            devices * per_owner * listed * 768 * 2 * len(comps), devices * rows * 1024
         ),
-    )(count, me, *[in_hbm(a) for a in (owner_row, slot_row, tiles)])
-
-
-def slab_kernel(comps, x_local, blocks, per_owner, table, twist, data, out, *scratch):
-    made, slab, turned, out_sems = scratch
+    )(count, me, *[in_hbm(a) for a in (owner_row, slot_row, tiles, *extra)])
+
+
+def complex_table(cos_part, sin_part):
+    return np.concatenate(
+        [
+            np.concatenate([cos_part, sin_part], axis=1),
+            np.concatenate([-sin_part, cos_part], axis=1),
+        ]
+    ).astype(np.float32)
+
+
+def slab_kernel(count, x_local, blocks, per_owner, first, table, twist, data, *refs):
+    if first:
+        out, landings, made, slab, turned, out_sems = refs
+    else:
+        landings, out, made, slab, turned, out_sems = refs
     devices = data.shape[0]
     entries = devices * per_owner
-    y_local = blocks * 128 // devices
-    wide = 2 * x_local
+    group = 128 // x_local
+    pairs = blocks // group
     shift = blocks.bit_length() - 1
-    every = 128 // per_owner
-    stated = [
-        sum([data[o, data.shape[1] - 8 :][:1] for o in range(start, start + every)])
-        for start in range(0, devices, every)
-    ]
-    slot = jnp.concatenate(stated, axis=1).astype(jnp.int32) - 1
-    landing = jnp.where(slot >= 0, (slot & (blocks - 1)) * x_local + (slot >> shift), -1)
+    if first:
+        every = 128 // per_owner
+        stated = [
+            sum([data[o, data.shape[1] - 8 :][:1] for o in range(start, start + every)])
+            for start in range(0, devices, every)
+        ]
+        slot = jnp.concatenate(stated, axis=1).astype(jnp.int32) - 1
+        landing = jnp.where(slot >= 0, (slot & (blocks - 1)) * x_local + (slot >> shift), -1)
+        landings[...] = landing
+    else:
+        landing = landings[...]
     parts = []
-    for comp in comps:
-        for r in range(2):
-            start = (2 * comp + r) * per_owner
-            one = data[:, start : start + per_owner, :]
-            parts.extend(split_two(one.reshape(entries, 128)))
+    for i in range(2 * count):
+        one = data[:, i * per_owner : (i + 1) * per_owner, :]
+        parts.extend(split_two(one.reshape(entries, 128)))
     parts = jnp.concatenate(parts, axis=1)
     for start in range(0, blocks * x_local, 256):
         place = start + lax.broadcasted_iota(jnp.int32, (256, entries), 0)
         chosen = jnp.where(place == landing, 1.0, 0.0).astype(jnp.bfloat16)
         got = jnp.dot(chosen, parts, preferred_element_type=jnp.float32)
-        for i in range(2 * len(comps)):
+        for i in range(2 * count):
             slab[i // 2, i % 2, start : start + 256, :] = (
                 got[:, 256 * i : 256 * i + 128] + got[:, 256 * i + 128 : 256 * i + 256]
             )
     sends = []
-    for index in range(len(comps)):
+    for index in range(count):
 
         @pl.loop(0, x_local // 8)
         def _(step):
@@ -243,26 +259,21 @@
             for k in range(blocks):
                 real, imag = waves[k]
                 cos_k, sin_k = twist[0, k : k + 1, :], twist[1, k : k + 1, :]
-                new_real = real * cos_k + imag * sin_k
-                new_imag = imag * cos_k - real * sin_k
-                first = pl.ds(k * wide + at, 8)
-                second = pl.ds(k * wide + x_local + at, 8)
-                turned[first, :128] = new_real
-                turned[first, 128:] = new_imag
-                turned[second, :128] = new_imag
-                turned[second, 128:] = -new_real
-
-        together = 4
-        for start in range(0, blocks, together):
-            moved = dot_rows_split(
-                table[...], turned[start * wide : (start + together) * wide, :]
-            )
-            for k in range(start, start + together):
-                one = moved[:, (k - start) * wide : (k - start + 1) * wide]
-                made[index, pl.ds(k, 128, stride=blocks), :] = one
+                rows = pl.ds(((k % pairs) * group + k // pairs) * x_local + at, 8)
+                turned[rows, :128] = real * cos_k + imag * sin_k
+                turned[rows, 128:] = imag * cos_k - real * sin_k
+
+        for start in range(0, pairs, 2):
+            moved = dot_rows_split(table[...], turned[start * 128 : (start + 2) * 128, :])
+            for k in range(2):
+                for r in range(2):
+                    rows = pl.ds(r * pairs + start + k, 128, stride=2 * pairs)
+                    made[index, rows, :] = moved[
+                        r * 128 : (r + 1) * 128, k * 128 : (k + 1) * 128
+                    ]
         send = pltpu.make_async_copy(
-            made.at[index].reshape(devices, y_local, wide),
-            out.at[:, pl.ds(index * y_local, y_local)],
+            made.at[index].reshape(devices, made.shape[1] // devices, 128),
+            out.at[:, index],
             out_sems.at[index],
         )
         send.start()
@@ -271,100 +282,131 @@
         send.wait()
 
 
-def slab_waves(comps, data, x_local, blocks, count_gl, per_owner):
+def slab_waves(data, landings, x_local, blocks, count_gl, per_owner):
     devices = data.shape[0]
-    y_cells = blocks * 128
-    y_local = y_cells // devices
+    count = data.shape[1] // (2 * per_owner)
+    first = landings is None
     fine = angles(128, 128, 128)
-    table = np.concatenate([np.cos(fine), np.sin(fine)], axis=1).astype(np.float32)
     order = owner_order(devices, count_gl)
-    table = table.reshape(devices, 128 // devices, 256)[order].reshape(128, 256)
-    twist_angle = angles(blocks, 128, y_cells)
+    fine = fine.reshape(devices, 128 // devices, 128)[order].reshape(128, 128)
+    table = complex_table(np.cos(fine), np.sin(fine))
+    twist_angle = angles(blocks, 128, blocks * 128)
     twist = np.stack([np.cos(twist_angle), np.sin(twist_angle)]).astype(np.float32)
     entries = devices * per_owner
-    count = len(comps)
+    rows = blocks * x_local * 2
+    out = pltpu.HBM((devices, count, rows // devices, 128), jnp.float32)
+    landing = jax.ShapeDtypeStruct((1, entries), jnp.int32)
+    in_place = pl.BlockSpec(memory_space=pltpu.VMEM)
     return pl.pallas_call(
-        functools.partial(slab_kernel, comps, x_local, blocks, per_owner),
-        out_shape=pltpu.HBM((devices, count * y_local, 2 * x_local), jnp.float32),
-        in_specs=[pl.BlockSpec(memory_space=pltpu.VMEM)] * 3,
-        out_specs=pl.BlockSpec(memory_space=pltpu.HBM),
+        functools.partial(slab_kernel, count, x_local, blocks, per_owner, first),
+        out_shape=(out, landing) if first else out,
+        in_specs=[in_place] * (3 if first else 4),
+        out_specs=(
+            (pl.BlockSpec(memory_space=pltpu.HBM), in_place)
+            if first
+            else pl.BlockSpec(memory_space=pltpu.HBM)
+        ),
         scratch_shapes=[
-            pltpu.VMEM((count, y_cells, 2 * x_local), jnp.float32),
+            pltpu.VMEM((count, rows, 128), jnp.float32),
             pltpu.VMEM((count, 2, blocks * x_local, 128), jnp.float32),
-            pltpu.VMEM((blocks * 2 * x_local, 256), jnp.float32),
+            pltpu.VMEM((blocks * x_local, 256), jnp.float32),
             pltpu.SemaphoreType.DMA((count,)),
         ],
         compiler_params=params(24),
         cost_estimate=cost(
-            count * (blocks * x_local * entries * 1024 + y_cells * x_local * 3072),
-            count * (entries * 1024 + y_cells * x_local * 8),
+            count * blocks * x_local * (entries * 1024 + 512 * 1024),
+            count * (entries * 1024 + rows * 512),
         ),
-    )(jnp.asarray(table), jnp.asarray(twist), in_vmem(data))
-
-
-def swap_parts(value, x_local):
-    if 2 * x_local == 128:
-        return pltpu.roll(value, x_local, 1)
-    return jnp.concatenate([value[:, x_local:], value[:, :x_local]], axis=1)
+    )(jnp.asarray(table), jnp.asarray(twist), in_vmem(data), *(() if first else (landings,)))
+
+
+def choose(options, mask_of):
+    made = options[0]
+    for i in range(1, len(options)):
+        made = jnp.where(mask_of(i), options[i], made)
+    return made
 
 
 def x_steps(
-    devices, x_local, y_local, order, index, twist, table, data, turned, columns, store
+    devices, x_local, y_local, blocks, order, index, twist, table, data, turned, columns, store
 ):
-    wide = 2 * x_local
-    lane = lax.broadcasted_iota(jnp.int32, (1, wide), 1)
-    sign = jnp.where(lane < x_local, 1.0, -1.0)
-
-    def times(value, k, length):
-        if k == 0:
-            return value
-        swapped = swap_parts(value, x_local) * sign
-        if 4 * k == length:
-            return swapped
-        cos_k = math.cos(2.0 * math.pi * k / length)
-        sin_k = math.sin(2.0 * math.pi * k / length)
-        return value * cos_k + swapped * sin_k
-
-    @pl.loop(0, y_local // 8)
+    group = 128 // x_local
+    pairs = blocks // group
+    kept = y_local // blocks
+    narrow = kept * pairs
+    banks = 2 * group
+
+    @pl.loop(0, kept)
     def _(step):
-        at = pl.multiple_of(step * 8, 8)
-        rows = pl.ds(index * y_local + at, 8)
-        values = [data[order.index(o), rows, :] for o in range(devices)]
-        waves = flat_fft(values, times)
+        at = pl.multiple_of(step * 2 * pairs, 2 * pairs)
+        values = [
+            tuple(
+                data[order.index(o), index, pl.ds(at + r * pairs, pairs), :] for r in range(2)
+            )
+            for o in range(devices)
+        ]
+        waves = flat_fft(values, times_pair)
+        rows = pl.ds(pl.multiple_of(step * pairs, pairs), pairs)
         for k in range(devices):
-            swapped = swap_parts(waves[k], x_local)
-            new = waves[k] * twist[0, k : k + 1, :] + swapped * twist[1, k : k + 1, :]
-            turned[k, pl.ds(at, 8), :] = new
-            turned[k, pl.ds(y_local + at, 8), :] = swap_parts(new, x_local) * sign
-
-    together = 4
+            real, imag = waves[k]
+            cos_k, sin_k = twist[0, k : k + 1, :], twist[1, k : k + 1, :]
+            turned[k, rows, :128] = real * cos_k + imag * sin_k
+            turned[k, rows, 128:] = imag * cos_k - real * sin_k
+
+    lane = lax.broadcasted_iota(jnp.int32, (1, 128), 1)
+    square = banks * narrow == 128 and 128 // narrow == banks
+    together = min(devices, 256 // narrow)
     for start in range(0, devices, together):
-        stacked = turned[start : start + together].reshape(together * 2 * y_local, wide)
+        stacked = turned[start : start + together].reshape(together * narrow, 256)
         moved = dot_rows_split(table[...], stacked)
-        for k in range(start, start + together):
-            columns[pl.ds(k, x_local, stride=devices), :] = moved[
-                :, (k - start) * 2 * y_local : (k - start + 1) * 2 * y_local
-            ]
+        if square:
+            for base in range(0, together, banks):
+                rolled = []
+                for bank in range(banks):
+                    one = moved[bank * x_local : (bank + 1) * x_local, base * narrow :][:, :128]
+                    rolled.append(pltpu.roll(one, bank * narrow, 1) if bank else one)
+                for k in range(banks):
+                    options = [rolled[(place - k) % banks] for place in range(banks)]
+                    rows = pl.ds(start + base + k, x_local, stride=devices)
+                    columns[rows, :] = choose(options, lambda i: lane // narrow == i)
+        else:
+            for k in range(together):
+                one = jnp.concatenate(
+                    [
+                        moved[bank * x_local : (bank + 1) * x_local, k * narrow : (k + 1) * narrow]
+                        for bank in range(banks)
+                    ],
+                    axis=1,
+                )
+                columns[pl.ds(start + k, x_local, stride=devices), :] = one
     for start in range(0, devices * x_local, 128):
-        store(start, columns[start : start + 128, :].T)
-
-
-def x_kernel(devices, x_local, y_local, order, index, twist, table, data, out, *scratch):
+        block = columns[start : start + 128, :].T
+        pieces = [block[bank * narrow : (bank + 1) * narrow] for bank in range(banks)]
+        for bank in range(banks):
+            one = pieces[bank]
+            if square:
+                options = [pieces[(bank + k) % banks] for k in range(banks)]
+                one = choose(options, lambda i: lane % banks == i)
+            for step in range(kept):
+                row = step * blocks + (bank % group) * pairs
+                store(bank // group, row, start, one[step * pairs : (step + 1) * pairs])
+
+
+def x_kernel(devices, x_local, y_local, blocks, order, index, twist, table, data, out, *scratch):
     made, out_sem = scratch[:2]
 
-    def store(start, block):
-        made[0, :, start : start + 128] = block[:y_local]
-        made[1, :, start : start + 128] = block[y_local:]
+    def store(r, row, start, block):
+        made[r, row : row + block.shape[0], start : start + 128] = block
 
     x_steps(
-        devices, x_local, y_local, order, index, twist, table, data, *scratch[2:], store
+        devices, x_local, y_local, blocks, order, index, twist, table, data, *scratch[2:], store
     )
     send = pltpu.make_async_copy(made, out, out_sem)
     send.start()
     send.wait()
 
 
-def last_kernel(devices, x_local, y_local, order, index, twist, table, data, *refs):
+def last_kernel(devices, x_local, y_local, blocks, order, index, twist, table, data, *refs):
     green, first, second, out = refs[:4]
     scratch, (tensor, kept, made, in_sems, out_sems) = refs[4:6], refs[6:]
     x_cells = devices * x_local
@@ -378,11 +420,12 @@
     for fetch in fetches:
         fetch.start()
 
-    def store(start, block):
-        kept[2, 0, :, start : start + 128] = block[:y_local]
-        kept[2, 1, :, start : start + 128] = block[y_local:]
-
-    x_steps(devices, x_local, y_local, order, index, twist, table, data, *scratch, store)
+    def store(r, row, start, block):
+        kept[2, r, row : row + block.shape[0], start : start + 128] = block
+
+    x_steps(
+        devices, x_local, y_local, blocks, order, index, twist, table, data, *scratch, store
+    )
     for fetch in fetches:
         fetch.wait()
     sends = []
@@ -426,20 +469,19 @@
 
 def x_tables(devices, x_local, y_cells):
     x_cells = devices * x_local
+    group = 128 // x_local
     fine = angles(x_local, x_local, x_local)
     scale = 1.0 / math.sqrt(x_cells * y_cells)
-    table = np.concatenate([np.cos(fine), np.sin(fine)], axis=1) * scale
-    angle = angles(devices, x_local, x_cells)
-    cos_a, sin_a = np.cos(angle), np.sin(angle)
-    twist = np.stack(
-        [np.concatenate([cos_a, cos_a], axis=1), np.concatenate([sin_a, -sin_a], axis=1)]
-    )
-    return jnp.asarray(twist.astype(np.float32)), jnp.asarray(table.astype(np.float32))
+    apart = np.eye(group) * scale
+    table = complex_table(np.kron(apart, np.cos(fine)), np.kron(apart, np.sin(fine)))
+    angle = np.tile(angles(devices, x_local, x_cells), (1, group))
+    twist = np.stack([np.cos(angle), np.sin(angle)]).astype(np.float32)
+    return jnp.asarray(twist), jnp.asarray(table)
 
 
 def x_scratch(devices, x_local, y_local):
     return [
-        pltpu.VMEM((devices, 2 * y_local, 2 * x_local), jnp.float32),
+        pltpu.VMEM((devices, y_local * x_local // 128, 256), jnp.float32),
         pltpu.VMEM((devices * x_local, 2 * y_local), jnp.float32),
     ]
 
@@ -448,7 +490,7 @@
     x_cells = devices * x_local
     order = owner_order(devices, count_gl)
     return pl.pallas_call(
-        functools.partial(x_kernel, devices, x_local, y_local, order, index),
+        functools.partial(x_kernel, devices, x_local, y_local, y_cells // 128, order, index),
         out_shape=pltpu.HBM((2, y_local, x_cells), jnp.float32),
         in_specs=[pl.BlockSpec(memory_space=pltpu.VMEM)] * 3,
         out_specs=pl.BlockSpec(memory_space=pltpu.HBM),
@@ -467,7 +509,7 @@
     order = owner_order(devices, count_gl)
     pieces = 8
     return pl.pallas_call(
-        functools.partial(last_kernel, devices, x_local, y_local, order, index),
+        functools.partial(last_kernel, devices, x_local, y_local, y_cells // 128, order, index),
         out_shape=pltpu.HBM((2, 3, y_local, x_cells), jnp.float32),
         in_specs=[pl.BlockSpec(memory_space=pltpu.VMEM)] * 3
         + [pl.BlockSpec(memory_space=pltpu.HBM)] * 3,
@@ -523,10 +565,14 @@
     green = green.reshape(2, 6, y_local, x_cells)
     me = (lax.axis_index("gx") * 4 + lax.axis_index("gz")) * count_gl + lax.axis_index("gl")
     lists = (owner_row, slot_row, tile_count, me.reshape(1).astype(jnp.int32))
-    arrived = exchange(pack(tiles, *lists, devices, count_gl, per_owner))
+    early = pack(tiles, (0, 1), *lists, None, devices, count_gl, per_owner)
+    late = pack(tiles, (2,), *lists, early, devices, count_gl, per_owner)
+    early = exchange(early)
+    late = exchange(once_after(late, early))
     grid = (x_local, blocks, count_gl, per_owner)
-    early = exchange(slab_waves((0, 1), arrived, *grid))
-    late = slab_waves((2,), arrived, *grid)
+    early, landings = slab_waves(early, None, *grid)
+    early = exchange(once_after(early, late))
+    late = slab_waves(late, landings, *grid)
     late = exchange(once_after(late, early))
     sizes = (devices, x_local, y_local, y_cells, count_gl)
     waves = [x_waves(comp, early, *sizes) for comp in range(2)]

time: 187 us -> 182 us (0.973)
  blocking collectives: 82.9 us -> 0 us
  waiting for transfers between devices: 56.9 us -> 134 us
  starting transfers between devices: 5.69 us -> 16 us
  Pallas kernels: 36.6 us -> 29.3 us
  local copies, waits for them, and re-layouts: 3.63 us -> 0.62 us
    all_to_all x1 -> x0, blocking collectives: 82.9 us -> none  [exchange(): lax.all_to_all(data, ('gx', 'gl', 'gz'), split_axis=0, concat_axis=0, til...]
    all_to_all x2 -> x4, waiting for transfers between devices: 56.9 us -> 134 us  [exchange(): lax.all_to_all(data, ('gx', 'gl', 'gz'), split_axis=0, concat_axis=0, til...]
    all_to_all x2 -> x4, starting transfers between devices: 5.69 us -> 16 us  [exchange(): lax.all_to_all(data, ('gx', 'gl', 'gz'), split_axis=0, concat_axis=0, til...]
    pallas_call x4, Pallas kernels: 22.6 us -> 15.3 us  [the longest x2 9.23 us: slab_waves(): pl.pallas_call(functools.partial(slab_kernel, count, x_local, blocks, per...]
    unnamed x12, local copies, waits for them, and re-layouts: 3.63 us -> 0.62 us
    pallas_call x1 -> x2, Pallas kernels: 6.1 us -> 8.07 us  [pack(): pl.pallas_call(functools.partial(pack_kernel, devices, count_gl, per_owne...]
    pallas_call x1, Pallas kernels: 7.86 us -> 5.96 us  [last_waves(): pl.pallas_call(functools.partial(last_kernel, devices, x_local, y_local,...]
  transfers between devices with their start and end apart: 2 -> 4, of which waited for: 2 -> 4; matrix products, arithmetic and copies ran while one was open for 0% -> 0% of each run, Pallas kernels for 9% -> 10%
where the time goes in v1:
time: 182 us; the launch traced here: 181 us
  waiting for transfers between devices  134 us (74%)
  Pallas kernels  29.3 us (16%)
  starting transfers between devices  16 us (9%)
    all_to_all x4, waiting for transfers between devices, exchange(): lax.all_to_all(data, ('gx', 'gl', 'gz'), split_axis=0, concat_axis=0, til...  134 us
    all_to_all x4, starting transfers between devices, exchange(): lax.all_to_all(data, ('gx', 'gl', 'gz'), split_axis=0, concat_axis=0, til...  16 us
    pallas_call x2, Pallas kernels, slab_waves(): pl.pallas_call(functools.partial(slab_kernel, count, x_local, blocks, per...  9.23 us
    pallas_call x2, Pallas kernels, pack(): pl.pallas_call(functools.partial(pack_kernel, devices, count_gl, per_owne...  8.07 us
    pallas_call x2, Pallas kernels, x_waves(): pl.pallas_call(functools.partial(x_kernel, devices, x_local, y_local, y_c...  6.07 us
    pallas_call x1, Pallas kernels, last_waves(): pl.pallas_call(functools.partial(last_kernel, devices, x_local, y_local,...  5.96 us
  transfers between devices with their start and end apart: 4, of which 4 were waited for; matrix products, arithmetic and copies ran while one was open for 0% of the time, Pallas kernels for 10%

profile of v1, /device:TPU:0, one launch (start us, length us, event | category | flops | bytes accessed | tf_op | source)
XLA Modules:
  0.0 181.1 jit_solution(5678877662864251168)
XLA Ops:
  0.7 4.8 %shard_map.145.refs_0_ = f32[32,136,128]{2,1,0:T(8,128)} custom-call(s32[1]{0:T(128)S(6)} %copy.23.count, s32[1]{0:T(128)} %bitcast.me, s32[1,512]{1,0:T(1,128)} %bitcast.8, s32[1,512]{1,0:T(1,128)} %bitcast.10, f32[2,3,512,128]{3,2,1,0:T(8,128)} %tiles.3), custom_call_target="tpu_custom_call" | custom-call | flops 1610612736 | bytes 4456448 | tf_op jit(solution)/shard_map/pallas_call | solution.py:185
  5.4 7.3 %all-to-all-start = ((f32[32,136,128]{2,1,0:T(8,128)}), f32[32,136,128]{2,1,0:T(8,128)S(1)}, u32[]{:S(2)}, u32[]{:S(2)}) async-start(f32[32,136,128]{2,1,0:T(8,128)} %shard_map.145.refs_0_), calls=%async_computation | async-start | bytes 4456448 | tf_op jit(solution)/shard_map/all_to_all | solution.py:551
  12.7 3.3 %shard_map.146.data = f32[32,64,128]{2,1,0:T(8,128)} custom-call(s32[1]{0:T(128)S(6)} %copy.23.count, s32[1]{0:T(128)} %bitcast.me, s32[1,512]{1,0:T(1,128)} %bitcast.9, s32[1,512]{1,0:T(1,128)} %bitcast.11, f32[2,3,512,128]{3,2,1,0:T(8,128)} %tiles.3, f32[32,136,128]{2,1,0:T(8,128)} %shard_map.145.refs_0_), custom_call_target="tpu_custom_call" | custom-call | flops 805306368 | bytes 2097152 | tf_op jit(solution)/shard_map/pallas_call | solution.py:185
  16.1 0.0 copy-start.2
  16.1 0.0 copy-start.3
  16.1 48.1 %all-to-all-done.after.data = f32[32,136,128]{2,1,0:T(8,128)S(1)} async-done(((f32[32,136,128]{2,1,0:T(8,128)}), f32[32,136,128]{2,1,0:T(8,128)S(1)}, u32[]{:S(2)}, u32[]{:S(2)}) %all-to-all-start) | async-done | bytes 2228256 | tf_op jit(solution)/shard_map/all_to_all | solution.py:551
  64.2 2.8 %all-to-all-start.1 = ((f32[32,64,128]{2,1,0:T(8,128)}), f32[32,64,128]{2,1,0:T(8,128)S(1)}, u32[]{:S(2)}, u32[]{:S(2)}) async-start(f32[32,64,128]{2,1,0:T(8,128)} %shard_map.147), calls=%async_computation.1 | async-start | bytes 2097152 | tf_op jit(solution)/shard_map/all_to_all | solution.py:551
  67.1 0.0 copy-done.2
  67.1 0.0 copy-done.3
  67.1 5.8 %shard_map.148 = (f32[32,2,64,128]{3,2,1,0:T(8,128)}, s32[1,1024]{1,0:T(1,128)S(1)}) custom-call(f32[256,256]{1,0:T(8,128)S(1)} %copy-done.2, f32[2,16,128]{2,1,0:T(8,128)S(1)} %copy-done.3, f32[32,136,128]{2,1,0:T(8,128)S(1)} %all-to-all-done.after.data), custom_call_target="tpu_custom_call" | custom-call | flops 3221225472 | bytes 4194304 | tf_op jit(solution)/shard_map/pallas_call | solution.py:300
  72.9 0.0 copy-start.4
  72.9 0.6 copy-done.4
  73.5 20.4 %all-to-all-done.1.data.after = f32[32,64,128]{2,1,0:T(8,128)S(1)} async-done(((f32[32,64,128]{2,1,0:T(8,128)}), f32[32,64,128]{2,1,0:T(8,128)S(1)}, u32[]{:S(2)}, u32[]{:S(2)}) %all-to-all-start.1) | async-done | bytes 1048608 | tf_op jit(solution)/shard_map/all_to_all | solution.py:551
  93.9 0.0 copy-start.5
  93.9 2.9 %all-to-all-start.2 = ((f32[32,2,64,128]{3,2,1,0:T(8,128)}), f32[32,2,64,128]{3,2,1,0:T(8,128)S(1)}, u32[]{:S(2)}, u32[]{:S(2)}) async-start(f32[32,2,64,128]{3,2,1,0:T(8,128)} %shard_map.150), calls=%async_computation.2 | async-start | bytes 4194304 | tf_op jit(solution)/shard_map/all_to_all | solution.py:551
  96.7 0.0 copy-done.5
  96.7 3.5 %shard_map.149.data = f32[32,1,64,128]{3,2,1,0:T(8,128)} custom-call(f32[256,256]{1,0:T(8,128)S(1)} %copy-done.2, f32[2,16,128]{2,1,0:T(8,128)S(1)} %copy-done.3, f32[32,64,128]{2,1,0:T(8,128)S(1)} %all-to-all-done.1.data.after, s32[1,1024]{1,0:T(1,128)S(1)} %copy-done.5), custom_call_target="tpu_custom_call" | custom-call | flops 1610612736 | bytes 2097152 | tf_op jit(solution)/shard_map/pallas_call | solution.py:300
  100.2 0.0 copy-start
  100.2 0.0 copy-start.1
  100.2 45.2 %all-to-all-done.2.after.data = f32[32,2,64,128]{3,2,1,0:T(8,128)S(1)} async-done(((f32[32,2,64,128]{3,2,1,0:T(8,128)}), f32[32,2,64,128]{3,2,1,0:T(8,128)S(1)}, u32[]{:S(2)}, u32[]{:S(2)}) %all-to-all-start.2) | async-done | bytes 2097184 | tf_op jit(solution)/shard_map/all_to_all | solution.py:551
  145.4 3.0 %all-to-all-start.3 = ((f32[32,1,64,128]{3,2,1,0:T(8,128)}), f32[32,1,64,128]{3,2,1,0:T(8,128)S(1)}, u32[]{:S(2)}, u32[]{:S(2)}) async-start(f32[32,1,64,128]{3,2,1,0:T(8,128)} %shard_map.151), calls=%async_computation.3 | async-start | bytes 2097152 | tf_op jit(solution)/shard_map/all_to_all | solution.py:551
  148.4 0.0 copy-done
  148.4 0.0 copy-done.1
  148.4 3.0 %shard_map.153.refs_2_ = f32[2,64,2048]{2,1,0:T(8,128)} custom-call(f32[2,32,128]{2,1,0:T(8,128)S(1)} %copy-done.1, f32[256,256]{1,0:T(8,128)S(1)} %copy-done, f32[32,2,64,128]{3,2,1,0:T(8,128)S(1)} %all-to-all-done.2.after.data), custom_call_target="tpu_custom_call" | custom-call | flops 201326592 | bytes 2097152 | tf_op jit(solution)/shard_map/pallas_call | solution.py:492
  151.4 3.0 %shard_map.152.refs_1_ = f32[2,64,2048]{2,1,0:T(8,128)} custom-call(f32[2,32,128]{2,1,0:T(8,128)S(1)} %copy-done.1, f32[256,256]{1,0:T(8,128)S(1)} %copy-done, f32[32,2,64,128]{3,2,1,0:T(8,128)S(1)} %all-to-all-done.2.after.data), custom_call_target="tpu_custom_call" | custom-call | flops 201326592 | bytes 2097152 | tf_op jit(solution)/shard_map/pallas_call | solution.py:492
  154.5 20.5 %all-to-all-done.3.data = f32[32,1,64,128]{3,2,1,0:T(8,128)S(1)} async-done(((f32[32,1,64,128]{3,2,1,0:T(8,128)}), f32[32,1,64,128]{3,2,1,0:T(8,128)S(1)}, u32[]{:S(2)}, u32[]{:S(2)}) %all-to-all-start.3) | async-done | bytes 1048608 | tf_op jit(solution)/shard_map/all_to_all | solution.py:551
  175.0 6.0 %shard_map.154 = f32[2,3,64,2048]{3,2,1,0:T(8,128)} custom-call(f32[2,32,128]{2,1,0:T(8,128)S(1)} %copy-done.1, f32[256,256]{1,0:T(8,128)S(1)} %copy-done, f32[32,1,64,128]{3,2,1,0:T(8,128)S(1)} %all-to-all-done.3.data, f32[2,6,64,2048]{3,2,1,0:T(8,128)} %bitcast.7, f32[2,64,2048]{2,1,0:T(8,128)} %shard_map.152.refs_1_, f32[2,64,2048]{2,1,0:T(8,128)} %shard_map.153.refs_2_), custom_call_target="tpu_custom_call" | custom-call | flops 210763776 | bytes 12582912 | tf_op jit(solution)/shard_map/pallas_call | solution.py:511
  (3 shorter events, 0.0 us)
Async XLA Ops:
  5.4 58.8 %all-to-all-start = ((f32[32,136,128]{2,1,0:T(8,128)}), f32[32,136,128]{2,1,0:T(8,128)S(1)}, u32[]{:S(2)}, u32[]{:S(2)}) async-start(f32[32,136,128]{2,1,0:T(8,128)} %shard_map.145.refs_0_), calls=%async_computation | async-start | bytes 4456448 | tf_op jit(solution)/shard_map/all_to_all | solution.py:551
  16.1 51.0 %copy-start.2 = (f32[256,256]{1,0:T(8,128)S(1)}, f32[256,256]{1,0:T(8,128)}, u32[]{:S(2)}) copy-start(f32[256,256]{1,0:T(8,128)} %constant.23.clone.table) | copy-start | bytes 786436
  16.1 51.0 %copy-start.3 = (f32[2,16,128]{2,1,0:T(8,128)S(1)}, f32[2,16,128]{2,1,0:T(8,128)}, u32[]{:S(2)}) copy-start(f32[2,16,128]{2,1,0:T(8,128)} %constant.24.clone.twist) | copy-start | bytes 49156
  64.2 29.6 %all-to-all-start.1 = ((f32[32,64,128]{2,1,0:T(8,128)}), f32[32,64,128]{2,1,0:T(8,128)S(1)}, u32[]{:S(2)}, u32[]{:S(2)}) async-start(f32[32,64,128]{2,1,0:T(8,128)} %shard_map.147), calls=%async_computation.1 | async-start | bytes 2097152 | tf_op jit(solution)/shard_map/all_to_all | solution.py:551
  72.9 0.6 copy-start.4
  93.9 2.9 %copy-start.5 = (s32[1,1024]{1,0:T(1,128)S(1)}, s32[1,1024]{1,0:T(1,128)}, u32[]{:S(2)}) copy-start(s32[1,1024]{1,0:T(1,128)} %copy-done.4) | copy-start | bytes 12292
  93.9 51.5 %all-to-all-start.2 = ((f32[32,2,64,128]{3,2,1,0:T(8,128)}), f32[32,2,64,128]{3,2,1,0:T(8,128)S(1)}, u32[]{:S(2)}, u32[]{:S(2)}) async-start(f32[32,2,64,128]{3,2,1,0:T(8,128)} %shard_map.150), calls=%async_computation.2 | async-start | bytes 4194304 | tf_op jit(solution)/shard_map/all_to_all | solution.py:551
  100.2 48.2 %copy-start = (f32[256,256]{1,0:T(8,128)S(1)}, f32[256,256]{1,0:T(8,128)}, u32[]{:S(2)}) copy-start(f32[256,256]{1,0:T(8,128)} %constant.26.clone.table) | copy-start | bytes 786436
  100.2 48.2 %copy-start.1 = (f32[2,32,128]{2,1,0:T(8,128)S(1)}, f32[2,32,128]{2,1,0:T(8,128)}, u32[]{:S(2)}) copy-start(f32[2,32,128]{2,1,0:T(8,128)} %constant.25.clone.twist) | copy-start | bytes 98308
  145.4 29.6 %all-to-all-start.3 = ((f32[32,1,64,128]{3,2,1,0:T(8,128)}), f32[32,1,64,128]{3,2,1,0:T(8,128)S(1)}, u32[]{:S(2)}, u32[]{:S(2)}) async-start(f32[32,1,64,128]{3,2,1,0:T(8,128)} %shard_map.151), calls=%async_computation.3 | async-start | bytes 2097152 | tf_op jit(solution)/shard_map/all_to_all | solution.py:551
